TPU v7x, 128 devices: a whole 4x4x4 slice. The times are simulated.
128 devices in a mesh: row: 16 (over z, y_lo, core), col: 8 (over x, y_hi).
Axes of the slice: x: 4, y: 4 (y_hi: 2, y_lo: 2; y = y_hi * 2 + y_lo), z: 4, core: 2. Of those that a mesh axis runs over, the one named last changes fastest.
Arguments:
- pair: bfloat16 [512, 512, 128], P('row', 'col'), may hold values from -6 to 6
- mask: int32 [512], replicated, may hold values 0 or 1
- out_in: bfloat16 [128, 512], replicated, may hold values from -0.5 to 0.5
- out_gate: bfloat16 [128, 128], replicated, may hold values from -0.5 to 0.5
- out_final: bfloat16 [128, 128], replicated, may hold values from -0.5 to 0.5
- in_in: bfloat16 [128, 512], replicated, may hold values from -0.5 to 0.5
- in_gate: bfloat16 [128, 128], replicated, may hold values from -0.5 to 0.5
- in_final: bfloat16 [128, 128], replicated, may hold values from -0.5 to 0.5
Outputs:
- updated: bfloat16 [512, 512, 128], P('row', 'col')
All inputs are finite; a program needn't handle non-finite values.
Results may differ from a plain program's by a relative error of at most 0.009.
Values may be sent and summed in bfloat16 or wider, within the bound.
A program may use at most 128 MiB of HBM per device.

v0:
```python
import jax
import jax.numpy as jnp
from jax import lax
from jax.sharding import PartitionSpec as P


def normalize(values):
    center = values - jnp.mean(values, axis=-1, keepdims=True)
    spread = jnp.mean(center * center, axis=-1, keepdims=True)
    return center * lax.rsqrt(spread + 1e-05)


def branch_inputs(tile, w_in, w_gate, pair_mask):
    normed = normalize(tile.astype(jnp.float32)).astype(jnp.bfloat16)
    proj = jnp.einsum("ijc,cd->ijd", normed, w_in, preferred_element_type=jnp.float32)
    width = w_gate.shape[0]
    weight = pair_mask[:, :, None]
    left = (weight * jax.nn.sigmoid(proj[..., 0:width]) * proj[..., width : 2 * width]).astype(
        jnp.bfloat16
    )
    right = (
        weight * jax.nn.sigmoid(proj[..., 2 * width : 3 * width]) * proj[..., 3 * width : 4 * width]
    ).astype(jnp.bfloat16)
    gate = jax.nn.sigmoid(
        jnp.einsum("ijc,cd->ijd", normed, w_gate, preferred_element_type=jnp.float32)
    )
    return (left, right, gate)


def finish(tile, total, gate, w_final):
    shaped = normalize(total).astype(jnp.bfloat16)
    branch = jnp.einsum("ijc,cd->ijd", shaped, w_final, preferred_element_type=jnp.float32)
    return (tile.astype(jnp.float32) + gate * branch).astype(jnp.bfloat16)


def shards(pair, mask, out_in, out_gate, out_final, in_in, in_gate, in_final):
    rows = pair.shape[0]
    cols = pair.shape[1]
    row_start = lax.axis_index("row") * rows
    col_start = lax.axis_index("col") * cols
    rows_mask = lax.dynamic_slice_in_dim(mask, row_start, rows).astype(jnp.float32)
    cols_mask = lax.dynamic_slice_in_dim(mask, col_start, cols).astype(jnp.float32)
    pair_mask = rows_mask[:, None] * cols_mask[None, :]
    left, right, gate = branch_inputs(pair, out_in, out_gate, pair_mask)
    left_first = left.transpose(2, 0, 1)
    right_rows = lax.all_gather(right.transpose(0, 2, 1), "row", axis=0, tiled=True)
    piece = right_rows
    summed = lax.psum_scatter(
        jnp.einsum("jck,cik->jci", piece, left_first, preferred_element_type=jnp.float32),
        "col",
        scatter_dimension=0,
        tiled=True,
    )
    total = summed.transpose(2, 0, 1)
    middle = finish(pair, total, gate, out_final)
    left, right, gate = branch_inputs(middle, in_in, in_gate, pair_mask)
    left_cols = lax.all_gather(left, "col", axis=1, tiled=True)
    piece = left_cols
    total = lax.psum_scatter(
        jnp.einsum("kic,kjc->ijc", piece, right, preferred_element_type=jnp.float32),
        "row",
        scatter_dimension=0,
        tiled=True,
    )
    return finish(middle, total, gate, in_final)


def solution(mesh):
    return jax.shard_map(
        shards,
        mesh=mesh,
        in_specs=(P("row", "col", None), P(), P(), P(), P(), P(), P(), P()),
        out_specs=P("row", "col", None),
        check_vma=False,
    )
```

profile of v0, /device:TPU:1, one launch (start us, length us, event | category | flops | bytes accessed | tf_op | source)
XLA Modules:
  0.0 541.4 jit_solution(16071332864267469369)
XLA Ops:
  8.1 1.4 convert_reduce_fusion.1
  9.5 1.7 fusion.16
  11.3 2.0 fusion.38
  13.2 1.4 fusion.58
  14.7 1.6 copy.45
  16.3 54.3 %all-gather.3.cloned.1.call-done = bf16[512,128,64]{1,2,0:T(8,128)(2,1)} async-done(((bf16[32,128,64]{1,2,0:T(8,128)(2,1)}), bf16[512,128,64]{1,2,0:T(8,128)(2,1)}) %all-gather.3.cloned.1.call-update) | async-done | bytes 8388624 | tf_op jit(solution)/shard_map/all_gather | solution.py:46
  70.6 23.7 %copy.46 = bf16[512,128,64]{2,0,1:T(8,128)(2,1)} copy(bf16[512,128,64]{1,2,0:T(8,128)(2,1)} %all-gather.3.cloned.1.call-done) | data formatting | bytes 16777216 | tf_op jit(solution)/shard_map/all_gather | solution.py:46
  94.3 14.6 %convolution_bitcast_fusion.1 = f32[512,128,32]{0,2,1:T(8,128)} fusion(bf16[128,32,64]{2,1,0:T(8,128)(2,1)S(1)} %copy.45, bf16[512,128,64]{2,0,1:T(8,128)(2,1)} %copy.46), kind=kOutput, calls=%fused_computation.1 | convolution fusion | flops 268435456 | bytes 17301504 | tf_op jit(solution)/shard_map/jck,cik->jci/dot_general | solution.py:49
  108.9 11.0 %copy.47 = f32[512,128,32]{1,2,0:T(8,128)} copy(f32[512,128,32]{0,2,1:T(8,128)} %convolution_bitcast_fusion.1) | data formatting | bytes 16777216 | tf_op jit(solution)/shard_map/jck,cik->jci/transpose | solution.py:49
  120.2 113.7 %reduce-scatter.3.cloned.1.call-done = f32[64,128,32]{1,2,0:T(8,128)} async-done(((f32[512,128,32]{1,2,0:T(8,128)}), f32[64,128,32]{1,2,0:T(8,128)}) %reduce-scatter.3.cloned.1.call-update) | async-done | bytes 1048592 | tf_op jit(solution)/shard_map/reduce_scatter | solution.py:48
  233.9 1.6 bitcast_reduce_fusion
  235.6 1.9 multiply_reduce_fusion.1
  237.7 1.8 multiply_convert_fusion.1
  242.5 1.4 fusion.18
  243.9 1.6 copy.53
  245.6 68.0 %all-gather.5.cloned.1.call-done = bf16[32,512,128]{2,1,0:T(8,128)(2,1)} async-done(((bf16[32,64,128]{2,1,0:T(8,128)(2,1)}), bf16[32,512,128]{2,1,0:T(8,128)(2,1)}) %all-gather.5.cloned.1.call-update) | async-done | bytes 4194320 | tf_op jit(solution)/shard_map/all_gather | solution.py:57
  313.6 7.9 %copy.54 = bf16[32,512,128]{1,0,2:T(8,128)(2,1)} copy(bf16[32,512,128]{2,1,0:T(8,128)(2,1)} %all-gather.5.cloned.1.call-done) | data formatting | bytes 8388608 | tf_op jit(solution)/shard_map/all_gather | solution.py:57
  321.5 10.3 %convolution_bitcast_fusion = f32[512,64,128]{0,1,2:T(8,128)} fusion(bf16[32,64,128]{1,0,2:T(8,128)(2,1)S(1)} %copy.53, bf16[32,512,128]{1,0,2:T(8,128)(2,1)} %copy.54), kind=kOutput, calls=%fused_computation | convolution fusion | flops 268435456 | bytes 21495808 | tf_op jit(solution)/shard_map/kic,kjc->ijc/dot_general | solution.py:60
  331.8 16.8 %copy.55 = f32[512,64,128]{2,1,0:T(8,128)} copy(f32[512,64,128]{0,1,2:T(8,128)} %convolution_bitcast_fusion) | data formatting | bytes 33554432 | tf_op jit(solution)/shard_map/kic,kjc->ijc/transpose | solution.py:60
  348.6 179.1 %reduce-scatter.5.cloned.1.call-done = f32[32,64,128]{2,1,0:T(8,128)} async-done(((f32[512,64,128]{2,1,0:T(8,128)}), f32[32,64,128]{2,1,0:T(8,128)}) %reduce-scatter.5.cloned.1.call-update) | async-done | bytes 1048592 | tf_op jit(solution)/shard_map/reduce_scatter | solution.py:59
  527.7 1.6 reduce_sum.78
  529.3 1.9 multiply_reduce_fusion
  531.2 1.9 fusion.44
  533.1 1.7 fusion.9
  (43 shorter events, 5.2 us)
Async XLA Ops:
  6.5 4.7 copy-start
  6.5 64.1 %all-gather.3.cloned.1.call-start = ((), (), s32[]{:S(2)}) async-start(), calls=%async_computation.2 | async-start | bytes 8912896 | tf_op jit(solution)/shard_map/all_gather | solution.py:46
  14.7 219.2 %reduce-scatter.3.cloned.1.call-start = ((), (), s32[]{:S(2)}) async-start(), calls=%async_computation.3 | async-start | bytes 9437184 | tf_op jit(solution)/shard_map/reduce_scatter | solution.py:48
  119.9 119.6 %copy-start.5 = (bf16[128,128]{1,0:T(8,128)(2,1)S(1)}, bf16[128,128]{1,0:T(8,128)(2,1)}, u32[]{:S(2)}) copy-start(bf16[128,128]{1,0:T(8,128)(2,1)} %param.12) | copy-start | bytes 98308
  119.9 119.9 %copy-start.2 = (bf16[32,64,128]{2,1,0:T(8,128)(2,1)S(1)}, bf16[32,64,128]{2,1,0:T(8,128)(2,1)}, u32[]{:S(2)}) copy-start(bf16[32,64,128]{2,1,0:T(8,128)(2,1)} %param.8) | copy-start | bytes 1572868
  119.9 119.9 %copy-start.6 = (bf16[128,128]{1,0:T(8,128)(2,1)S(1)}, bf16[128,128]{1,0:T(8,128)(2,1)}, u32[]{:S(2)}) copy-start(bf16[128,128]{1,0:T(8,128)(2,1)} %param.11) | copy-start | bytes 98308
  119.9 121.8 %copy-start.3 = (bf16[128,512]{1,0:T(8,128)(2,1)S(1)}, bf16[128,512]{1,0:T(8,128)(2,1)}, u32[]{:S(2)}) copy-start(bf16[128,512]{1,0:T(8,128)(2,1)} %param.13) | copy-start | bytes 393220
  119.9 193.6 %all-gather.5.cloned.1.call-start = ((), (), s32[]{:S(2)}) async-start(), calls=%async_computation.4 | async-start | bytes 4718592 | tf_op jit(solution)/shard_map/all_gather | solution.py:57
  243.9 283.8 %reduce-scatter.5.cloned.1.call-start = ((), (), s32[]{:S(2)}) async-start(), calls=%async_computation.5 | async-start | bytes 17825792 | tf_op jit(solution)/shard_map/reduce_scatter | solution.py:59
  348.5 182.6 %copy-start.4 = (bf16[128,128]{1,0:T(8,128)(2,1)S(1)}, bf16[128,128]{1,0:T(8,128)(2,1)}, u32[]{:S(2)}) copy-start(bf16[128,128]{1,0:T(8,128)(2,1)} %param.15) | copy-start | bytes 98308
  348.5 184.6 %copy-start.7 = (bf16[128,128]{1,0:T(8,128)(2,1)S(1)}, bf16[128,128]{1,0:T(8,128)(2,1)}, u32[]{:S(2)}) copy-start(bf16[128,128]{1,0:T(8,128)(2,1)} %param.14) | copy-start | bytes 98308
  348.6 186.3 %copy-start.1 = (bf16[128,512]{1,0:T(8,128)(2,1)S(1)}, bf16[128,512]{1,0:T(8,128)(2,1)}, u32[]{:S(2)}) copy-start(bf16[128,512]{1,0:T(8,128)(2,1)} %param.10) | copy-start | bytes 393220
Sparse Core Ops, SparseCore 0:
  14.8 55.7 all-gather.2
  120.1 113.7 reduce-scatter.2
  244.0 69.4 all-gather.4
  348.7 178.9 reduce-scatter.4
where the time goes:
time: 544 us; the launch traced here: 541 us
  waiting for transfers between devices  415 us (76%)
  local copies, waits for them, and re-layouts  63 us (12%)
  matrix products  32.7 us (6%)
  other arithmetic  16.9 us (3%)
  between operations  13.3 us (2%)
    reduce_scatter x1, waiting for transfers between devices, shards(): lax.psum_scatter(jnp.einsum('kic,kjc->ijc', piece, right, preferred_eleme...  179 us
    reduce_scatter x1, waiting for transfers between devices, shards(): lax.psum_scatter(jnp.einsum('jck,cik->jci', piece, left_first, preferred_...  114 us
    all_gather x1, waiting for transfers between devices, shards(): left_cols = lax.all_gather(left, 'col', axis=1, tiled=True)  68 us
    all_gather x1, waiting for transfers between devices, shards(): lax.all_gather(right.transpose(0, 2, 1), 'row', axis=0, tiled=True)  54.3 us
    all_gather x1, local copies, waits for them, and re-layouts, shards(): lax.all_gather(right.transpose(0, 2, 1), 'row', axis=0, tiled=True)  23.7 us
    transpose x1, local copies, waits for them, and re-layouts, shards(): jnp.einsum('kic,kjc->ijc', piece, right, preferred_element_type=jnp.float32)  16.8 us
    dot_general x1, matrix products, shards(): jnp.einsum('jck,cik->jci', piece, left_first, preferred_element_type=jnp....  14.6 us
    transpose x1, local copies, waits for them, and re-layouts, shards(): jnp.einsum('jck,cik->jci', piece, left_first, preferred_element_type=jnp....  11 us
  transfers between devices with their start and end apart: 4, of which 4 were waited for; matrix products, arithmetic and copies ran while one was open for 1% of the time, Pallas kernels for 0%

commit v1 on v0

v1 whole, which is shorter than its diff:
```python
import functools

import jax
import jax.numpy as jnp
from jax import lax
from jax.experimental import pallas as pl
from jax.experimental.pallas import tpu as pltpu
from jax.sharding import PartitionSpec as P

MESH = pl.DeviceIdType.MESH
CH = 128
S = 16
L = 128
DEVS = 128
ROWS = 16
COLS = 8
SCRAMBLE = 37
BF = jnp.bfloat16
F32 = jnp.float32


def place(t):
    row, col = lax.axis_index("row"), lax.axis_index("col")
    x = lax.rem(col // 2 + lax.rem(t // 2, 4), 4)
    y = lax.rem(lax.rem(col, 2) * 2 + lax.rem(row // 2, 2) + lax.rem(t // 8, 4), 4)
    z = lax.rem(row // 4 + t // 32, 4)
    core = lax.rem(lax.rem(row, 2) + lax.rem(t, 2), 2)
    to_row = z * 4 + lax.rem(y, 2) * 2 + core
    to_col = x * 2 + y // 2
    return to_row, to_col, to_row * COLS + to_col


def sigmoid(v):
    return 0.5 * jnp.tanh(0.5 * v) + 0.5


def norm0(v):
    center = v - jnp.mean(v, axis=0, keepdims=True)
    spread = jnp.mean(center * center, axis=0, keepdims=True)
    return center * lax.rsqrt(spread + 1e-05)


def swap_halves(first, second):
    low = lax.broadcasted_iota(jnp.int32, first.shape, 1) < 64
    return (
        jnp.where(low, first, pltpu.roll(second, 64, 1)),
        jnp.where(low, pltpu.roll(first, 64, 1), second),
    )


def exchange(send, recv, sems, me):
    send_sem, recv_sem = sems

    @pl.loop(1, DEVS)
    def _(t):
        to_row, to_col, to = place(lax.rem(t * SCRAMBLE, DEVS))
        pltpu.make_async_remote_copy(
            src_ref=send.at[to],
            dst_ref=recv.at[me],
            send_sem=send_sem,
            recv_sem=recv_sem,
            device_id=(to_row, to_col),
            device_id_type=MESH,
        ).start()

    recv[me] = send[me]


def arrived(send, recv, sems):
    others = pl.ds(0, DEVS - 1)
    pltpu.make_async_copy(recv.at[others], recv.at[others], sems[1]).wait()


def sent(send, recv, sems):
    others = pl.ds(0, DEVS - 1)
    pltpu.make_async_copy(send.at[others], send.at[others], sems[0]).wait()


def branch_inputs(q, values, weights, mask, gate, left, right):
    normed = norm0(values).astype(BF)
    proj = jnp.dot(weights[...], normed, preferred_element_type=F32)
    keep = jnp.concatenate([mask[pl.ds(2 * q, 1), :], mask[pl.ds(2 * q + 1, 1), :]], axis=1)
    lv = keep * sigmoid(proj[0:CH]) * proj[CH : 2 * CH]
    rv = keep * sigmoid(proj[2 * CH : 3 * CH]) * proj[3 * CH : 4 * CH]
    gate[q] = sigmoid(proj[4 * CH : 5 * CH])
    for e in range(2):
        rows = pl.ds(2 * q + e, CH, stride=S)
        left[rows, :] = lv[:, e * L : (e + 1) * L]
        right[rows, :] = rv[:, e * L : (e + 1) * L]


def pack(left, right, send):
    @pl.loop(0, CH // 16)
    def _(g):
        rows = pl.ds(pl.multiple_of(g * 256, 256), 256)
        chans = pl.ds(g * 16, 16)
        send[chans, 0:S, :] = left[rows, :].reshape(16, S, L).astype(BF)
        send[chans, S : 2 * S, :] = right[rows, :].reshape(16, S, L).astype(BF)


def multiply(recv, lmat, rmat, send, dims):
    @pl.loop(0, ROWS)
    def _(r):
        for part, mat in ((0, lmat), (1, rmat)):
            for p in range(COLS // 2):
                first = recv[r * COLS + 2 * p, part * S : (part + 1) * S, :]
                second = recv[r * COLS + 2 * p + 1, part * S : (part + 1) * S, :]
                low, high = swap_halves(first, second)
                at = pl.multiple_of(r * 2 * S, 2 * S)
                mat[pl.ds(at, S), p * L : (p + 1) * L] = low
                mat[pl.ds(at + S, S), p * L : (p + 1) * L] = high

    for block in range(4):
        rows = slice(block * 128, (block + 1) * 128)
        part = lmat[rows, :] if dims == 1 else lmat[:, rows]
        total = lax.dot_general(
            part, rmat[...], (((dims,), (dims,)), ((), ())), preferred_element_type=F32
        ).astype(BF)
        for k in range(4):
            r = block * 4 + k
            for p in range(COLS // 2):
                cols = slice(p * L, (p + 1) * L)
                low, high = swap_halves(
                    total[k * 2 * S : k * 2 * S + S, cols], total[k * 2 * S + S : (k + 1) * 2 * S, cols]
                )
                send[r * COLS + 2 * p] = low
                send[r * COLS + 2 * p + 1] = high


def shape(recv, wide):
    total = jnp.zeros((S, L), F32)
    total = lax.fori_loop(0, 8, lambda g, a: a + jnp.sum(recv[pl.ds(g * 16, 16)].astype(F32), axis=0), total)
    mean = total * (1.0 / CH)

    def squares(g, a):
        center = recv[pl.ds(g * 16, 16)].astype(F32) - mean[None]
        return a + jnp.sum(center * center, axis=0)

    spread = lax.fori_loop(0, 8, squares, jnp.zeros((S, L), F32)) * (1.0 / CH)
    scale = lax.rsqrt(spread + 1e-05)

    @pl.loop(0, 8)
    def _(g):
        rows = pl.ds(pl.multiple_of(g * 256, 256), 256)
        wide[rows, :] = ((recv[pl.ds(g * 16, 16)].astype(F32) - mean[None]) * scale[None]).reshape(256, L)


def finish(q, wide, weights, gate, base):
    shaped = jnp.concatenate(
        [wide[pl.ds(2 * q + e, CH, stride=S), :] for e in range(2)], axis=1
    ).astype(BF)
    branch = jnp.dot(weights[...], shaped, preferred_element_type=F32)
    return (base[q].astype(F32) + gate[q] * branch).astype(BF)


def kernel(
    pair, mask, in1, gate1, final1, in2, gate2, final2, out,
    base, gate, left, right, wt, ft, keep,
    send_a, recv_a, send_b, recv_b, send_c, recv_c, send_d, recv_d, lmat, rmat, send_sems, recv_sems,
):
    row, col = lax.axis_index("row"), lax.axis_index("col")
    me = row * COLS + col
    sems = [(send_sems.at[k], recv_sems.at[k]) for k in range(4)]

    barrier = pltpu.get_barrier_semaphore()

    @pl.loop(1, DEVS)
    def _(t):
        to_row, to_col, _ = place(t)
        pl.semaphore_signal(barrier, inc=1, device_id=(to_row, to_col), device_id_type=MESH)

    for k, (a, b, c) in enumerate(((in1, gate1, final1), (in2, gate2, final2))):
        wt[k, 0 : 4 * CH] = a[...].astype(F32).T.astype(BF)
        wt[k, 4 * CH : 5 * CH] = b[...].astype(F32).T.astype(BF)
        ft[k] = c[...].astype(F32).T.astype(BF)

    held = mask[...].astype(F32)
    spot = lax.broadcasted_iota(jnp.int32, (S, 512), 1)
    line = lax.broadcasted_iota(jnp.int32, (S, 512), 0)
    first = jnp.sum(jnp.where(spot == row * 32 + line, held, 0.0), axis=1, keepdims=True)
    second = jnp.sum(jnp.where(spot == row * 32 + 16 + line, held, 0.0), axis=1, keepdims=True)
    spot = lax.broadcasted_iota(jnp.int32, (L, 512), 1)
    line = lax.broadcasted_iota(jnp.int32, (L, 512), 0)
    across = jnp.sum(
        jnp.where(spot == col * 64 + lax.rem(line, 64), held, 0.0), axis=1, keepdims=True
    )
    across = jnp.broadcast_to(across, (L, L)).T[0:S]
    lane = lax.broadcasted_iota(jnp.int32, (S, L), 1)
    keep[...] = jnp.where(lane < 64, first, second) * across

    @pl.loop(0, S // 2)
    def _(q):
        values = jnp.concatenate(
            [pair[2 * q], pair[S + 2 * q], pair[2 * q + 1], pair[S + 2 * q + 1]], axis=0
        )
        values = values.astype(F32).T
        base[q] = values.astype(BF)
        branch_inputs(q, values, wt.at[0], keep, gate, left, right)

    pack(left, right, send_a)
    pl.semaphore_wait(barrier, DEVS - 1)
    exchange(send_a, recv_a, sems[0], me)
    arrived(send_a, recv_a, sems[0])
    multiply(recv_a, lmat, rmat, send_b, 1)
    exchange(send_b, recv_b, sems[1], me)
    arrived(send_b, recv_b, sems[1])
    shape(recv_b, left)

    @pl.loop(0, S // 2)
    def _(q):
        middle = finish(q, left, ft.at[0], gate, base)
        base[q] = middle
        branch_inputs(q, middle.astype(F32), wt.at[1], keep, gate, left, right)

    pack(left, right, send_c)
    exchange(send_c, recv_c, sems[2], me)
    arrived(send_c, recv_c, sems[2])
    multiply(recv_c, lmat, rmat, send_d, 0)
    exchange(send_d, recv_d, sems[3], me)
    arrived(send_d, recv_d, sems[3])
    shape(recv_d, left)

    @pl.loop(0, S // 2)
    def _(q):
        done = finish(q, left, ft.at[1], gate, base).astype(F32).T.astype(BF)
        out[2 * q] = done[0:64]
        out[S + 2 * q] = done[64:128]
        out[2 * q + 1] = done[128:192]
        out[S + 2 * q + 1] = done[192:256]

    for k, (a, b) in enumerate(((send_a, recv_a), (send_b, recv_b), (send_c, recv_c), (send_d, recv_d))):
        sent(a, b, sems[k])


def shards(pair, mask, *weights):
    vmem = pl.BlockSpec(memory_space=pltpu.VMEM)
    two = pltpu.VMEM((DEVS, 2 * S, L), BF)
    one = pltpu.VMEM((DEVS, S, L), BF)
    return pl.pallas_call(
        kernel,
        out_shape=jax.ShapeDtypeStruct(pair.shape, BF),
        in_specs=[vmem] * 8,
        out_specs=vmem,
        scratch_shapes=[
            pltpu.VMEM((S // 2, CH, 2 * L), BF),
            pltpu.VMEM((S // 2, CH, 2 * L), F32),
            pltpu.VMEM((CH * S, L), F32),
            pltpu.VMEM((CH * S, L), F32),
            pltpu.VMEM((2, 5 * CH, CH), BF),
            pltpu.VMEM((2, CH, CH), BF),
            pltpu.VMEM((S, L), F32),
            two, two, one, one, two, two, one, one,
            pltpu.VMEM((512, 512), BF),
            pltpu.VMEM((512, 512), BF),
            pltpu.SemaphoreType.DMA((4,)),
            pltpu.SemaphoreType.DMA((4,)),
        ],
        compiler_params=pltpu.CompilerParams(
            collective_id=0, has_side_effects=True, vmem_limit_bytes=48 * 2**20
        ),
    )(pair, mask.reshape(1, 512), *weights)


def solution(mesh):
    return jax.shard_map(
        shards,
        mesh=mesh,
        in_specs=(P("row", "col", None), P(), P(), P(), P(), P(), P(), P()),
        out_specs=P("row", "col", None),
        check_vma=False,
    )
```

time: 544 us -> 86.5 us (0.16)
  waiting for transfers between devices: 415 us -> 0 us
  Pallas kernels: 0 us -> 78.6 us
  local copies, waits for them, and re-layouts: 63 us -> 7.35 us
  matrix products: 32.7 us -> 0 us
  other arithmetic: 16.9 us -> 0 us
  between operations: 13.3 us -> 0.02 us
    reduce_scatter x2 -> x0, waiting for transfers between devices: 293 us -> none  [the longest x1 179 us: shards(): lax.psum_scatter(jnp.einsum('kic,kjc->ijc', piece, right, preferred_eleme...]
    all_gather x2 -> x0, waiting for transfers between devices: 122 us -> none  [the longest x1 68 us: shards(): left_cols = lax.all_gather(left, 'col', axis=1, tiled=True)]
    pallas_call x0 -> x1, Pallas kernels: none -> 78.6 us  [shards(): pl.pallas_call(kernel, out_shape=jax.ShapeDtypeStruct(pair.shape, BF), in...]
    dot_general x8 -> x0, matrix products: 32.7 us -> none  [the longest x1 14.6 us: shards(): jnp.einsum('jck,cik->jci', piece, left_first, preferred_element_type=jnp....]
    all_gather x2 -> x0, local copies, waits for them, and re-layouts: 31.6 us -> none  [the longest x1 23.7 us: shards(): lax.all_gather(right.transpose(0, 2, 1), 'row', axis=0, tiled=True)]
    transpose x3 -> x0, local copies, waits for them, and re-layouts: 29.4 us -> none  [the longest x1 16.8 us: shards(): jnp.einsum('kic,kjc->ijc', piece, right, preferred_element_type=jnp.float32)]
    reduce_sum x7 -> x0, other arithmetic: 10.6 us -> none  [the longest x4 6.06 us: normalize(): spread = jnp.mean(center * center, axis=-1, keepdims=True)]
    unnamed x16 -> x17, local copies, waits for them, and re-layouts: 0.03 us -> 7.35 us
  transfers between devices with their start and end apart: 4 -> 0, of which waited for: 4 -> 0; matrix products, arithmetic and copies ran while one was open for 1% -> 0% of each run, Pallas kernels for 0% -> 0%
where the time goes in v1:
time: 86.5 us; the launch traced here: 86 us
  Pallas kernels  78.6 us (91%)
  local copies, waits for them, and re-layouts  7.35 us (8%)
    pallas_call x1, Pallas kernels, shards(): pl.pallas_call(kernel, out_shape=jax.ShapeDtypeStruct(pair.shape, BF), in...  78.6 us
    unnamed x17, local copies, waits for them, and re-layouts  7.35 us

profile of v1, /device:TPU:1, one launch (start us, length us, event | category | flops | bytes accessed | tf_op | source)
XLA Modules:
  0.0 86.0 jit_solution(12950425596065771912)
XLA Ops:
  0.0 0.0 copy-start
  0.0 1.0 %copy-done = bf16[32,64,128]{2,1,0:T(8,128)(2,1)S(1)} copy-done((bf16[32,64,128]{2,1,0:T(8,128)(2,1)S(1)}, bf16[32,64,128]{2,1,0:T(8,128)(2,1)}, u32[]{:S(2)}) %copy-start) | copy-done | bytes 524312
  1.0 0.0 copy-start.1
  1.0 0.9 %copy-done.1 = bf16[128,512]{1,0:T(8,128)(2,1)S(1)} copy-done((bf16[128,512]{1,0:T(8,128)(2,1)S(1)}, bf16[128,512]{1,0:T(8,128)(2,1)}, u32[]{:S(2)}) %copy-start.1) | copy-done | bytes 131096
  1.9 0.0 copy-start.2
  1.9 0.9 %copy-done.2 = bf16[128,512]{1,0:T(8,128)(2,1)S(1)} copy-done((bf16[128,512]{1,0:T(8,128)(2,1)S(1)}, bf16[128,512]{1,0:T(8,128)(2,1)}, u32[]{:S(2)}) %copy-start.2) | copy-done | bytes 131096
  2.9 0.0 copy-start.3
  2.9 0.8 copy-done.3
  3.6 0.0 copy-start.4
  3.6 0.8 copy-done.4
  4.4 0.0 copy-start.5
  4.4 0.8 copy-done.5
  5.1 0.0 copy-start.6
  5.1 0.8 copy-done.6
  5.9 0.0 copy-start.7
  5.9 0.7 copy-done.7
  6.6 78.6 %shard_map.82 = bf16[32,64,128]{2,1,0:T(8,128)(2,1)S(1)} custom-call(bf16[32,64,128]{2,1,0:T(8,128)(2,1)S(1)} %copy-done, s32[1,512]{1,0:T(1,128)S(1)} %bitcast.1, bf16[128,512]{1,0:T(8,128)(2,1)S(1)} %copy-done.1, bf16[128,128]{1,0:T(8,128)(2,1)S(1)} %copy-done.3, bf16[128,128]{1,0:T(8,128)(2,1)S(1)} %copy-done.4, bf16[128,512]{1,0:T(8,128)(2,1)S(1)} %copy-done.2, ...), custom_call_target="tpu_custom_call" | custom-call | tf_op jit(solution)/shard_map/pallas_call | solution.py:239
  85.2 0.8 copy.10
Async XLA Ops:
  0.0 1.0 %copy-start = (bf16[32,64,128]{2,1,0:T(8,128)(2,1)S(1)}, bf16[32,64,128]{2,1,0:T(8,128)(2,1)}, u32[]{:S(2)}) copy-start(bf16[32,64,128]{2,1,0:T(8,128)(2,1)} %pair.1) | copy-start | bytes 1572868
  1.0 0.9 %copy-start.1 = (bf16[128,512]{1,0:T(8,128)(2,1)S(1)}, bf16[128,512]{1,0:T(8,128)(2,1)}, u32[]{:S(2)}) copy-start(bf16[128,512]{1,0:T(8,128)(2,1)} %in1.1) | copy-start | bytes 393220
  1.9 0.9 %copy-start.2 = (bf16[128,512]{1,0:T(8,128)(2,1)S(1)}, bf16[128,512]{1,0:T(8,128)(2,1)}, u32[]{:S(2)}) copy-start(bf16[128,512]{1,0:T(8,128)(2,1)} %in2.1) | copy-start | bytes 393220
  2.9 0.8 copy-start.3
  3.6 0.8 copy-start.4
  4.4 0.8 copy-start.5
  5.1 0.8 copy-start.6
  5.9 0.7 copy-start.7

commit v2 on v1

v2 whole, which is shorter than its diff:
```python
import jax
import jax.numpy as jnp
from jax import lax
from jax.experimental import pallas as pl
from jax.experimental.pallas import tpu as pltpu
from jax.sharding import PartitionSpec as P

VMEM_BYTES = 63 * 2**20
UNROLL = True
LOGICAL = pl.DeviceIdType.LOGICAL
CH = 128
S = 16
L = 128
DEVS = 128
ROWS = 16
COLS = 8
BF = jnp.bfloat16
F32 = jnp.float32
PLANE = sorted(
    ((dx, dy, dc) for dx in range(4) for dy in range(4) for dc in range(2)),
    key=lambda o: -min(o[0], 4 - o[0]) - min(o[1], 4 - o[1]),
)
ORDER = sorted(
    ((dx, dy, dz, dc) for dz in range(4) for dy in range(4) for dx in range(4) for dc in range(2)),
    key=lambda o: -sum(min(v, 4 - v) for v in o[:3]),
)[:-2] + [(0, 0, 0, 1)]


class Torus:
    def __init__(self):
        row, col = lax.axis_index("row"), lax.axis_index("col")
        self.me = row * COLS + col
        self.z = row // 4
        y = lax.rem(col, 2) * 2 + lax.rem(row // 2, 2)
        self.planes = [lax.rem(self.z + d, 4) for d in range(4)]
        ys = [lax.rem(y + d, 4) for d in range(4)]
        self.ys = [lax.rem(v, 2) * 16 + v // 2 for v in ys]
        self.xs = [lax.rem(col // 2 + d, 4) * 2 for d in range(4)]
        self.cs = [lax.rem(lax.rem(row, 2) + d, 2) * 8 for d in range(2)]

    def at(self, dx, dy, dz, dc):
        return self.planes[dz] * 32 + self.ys[dy] + self.xs[dx] + self.cs[dc]


def sigmoid(v):
    return 0.5 * jnp.tanh(0.5 * v) + 0.5


def norm0(v):
    center = v - jnp.mean(v, axis=0, keepdims=True)
    spread = jnp.mean(center * center, axis=0, keepdims=True)
    return center * lax.rsqrt(spread + 1e-05)


def swap_halves(first, second):
    low = lax.broadcasted_iota(jnp.int32, first.shape, 1) < 64
    return (
        jnp.where(low, first, pltpu.roll(second, 64, 1)),
        jnp.where(low, pltpu.roll(first, 64, 1), second),
    )


def push(torus, to, send, recv, sems):
    pltpu.make_async_remote_copy(
        src_ref=send.at[to],
        dst_ref=recv.at[torus.me],
        send_sem=sems[0],
        recv_sem=sems[1],
        device_id=to,
        device_id_type=LOGICAL,
    ).start()


def exchange(torus, send, recv, sems):
    for offset in ORDER:
        push(torus, torus.at(*offset), send, recv, sems)
    recv[torus.me] = send[torus.me]


def wait_all(ref, sem):
    others = ref.at[pl.ds(0, DEVS - 1)]
    pltpu.make_async_copy(others, others, sem).wait()


def edge(side, weights, normed, keep, wide, send):
    @pl.loop(0, S // 2, unroll=UNROLL)
    def _(q):
        proj = jnp.dot(
            weights[side * 2 * CH : (side + 1) * 2 * CH, :], normed[q], preferred_element_type=F32
        )
        mask = jnp.concatenate([keep[pl.ds(2 * q, 1), :], keep[pl.ds(2 * q + 1, 1), :]], axis=1)
        value = mask * sigmoid(proj[0:CH]) * proj[CH : 2 * CH]
        for e in range(2):
            wide[pl.ds(2 * q + e, CH, stride=S), :] = value[:, e * L : (e + 1) * L]

    @pl.loop(0, CH // 16, unroll=UNROLL)
    def _(g):
        rows = pl.ds(pl.multiple_of(g * 256, 256), 256)
        send[pl.ds(g * 16, 16)] = wide[rows, :].reshape(16, S, L).astype(BF)


def gates(weights, normed, gate):
    @pl.loop(0, S // 2, unroll=UNROLL)
    def _(q):
        gate[q] = sigmoid(
            jnp.dot(weights[4 * CH : 5 * CH, :], normed[q], preferred_element_type=F32)
        )


def gather(recv, mat, turned):
    @pl.loop(0, ROWS, unroll=UNROLL)
    def _(r):
        at = pl.multiple_of(r * 2 * S, 2 * S)
        for p in range(COLS // 2):
            low, high = swap_halves(recv[r * COLS + 2 * p], recv[r * COLS + 2 * p + 1])
            mat[pl.ds(at, S), p * L : (p + 1) * L] = low
            mat[pl.ds(at + S, S), p * L : (p + 1) * L] = high

    if turned is not None:
        for m in range(4):
            for n in range(4):
                turned[n * L : (n + 1) * L, m * L : (m + 1) * L] = mat[
                    m * L : (m + 1) * L, n * L : (n + 1) * L
                ].T


def multiply(torus, lhs, rhs, send, recv, sems):
    for dz in (2, 1, 3, 0):
        plane = torus.planes[dz]
        total = jnp.dot(
            lhs[pl.ds(pl.multiple_of(plane * L, L), L), :], rhs[...], preferred_element_type=F32
        ).astype(BF)
        for k in range(4):
            for p in range(COLS // 2):
                cols = slice(p * L, (p + 1) * L)
                low, high = swap_halves(
                    total[k * 2 * S : k * 2 * S + S, cols],
                    total[k * 2 * S + S : (k + 1) * 2 * S, cols],
                )
                send[plane * 32 + k * COLS + 2 * p] = low
                send[plane * 32 + k * COLS + 2 * p + 1] = high
        for dx, dy, dc in PLANE:
            if (dx, dy, dz, dc) != (0, 0, 0, 0):
                push(torus, torus.at(dx, dy, dz, dc), send, recv, sems)
    recv[torus.me] = send[torus.me]


def shape(recv, wide):
    total = lax.fori_loop(
        0, 8, lambda g, a: a + jnp.sum(recv[pl.ds(g * 16, 16)].astype(F32), axis=0), jnp.zeros((S, L), F32), unroll=UNROLL
    )
    mean = total * (1.0 / CH)

    def squares(g, a):
        center = recv[pl.ds(g * 16, 16)].astype(F32) - mean[None]
        return a + jnp.sum(center * center, axis=0)

    spread = lax.fori_loop(0, 8, squares, jnp.zeros((S, L), F32), unroll=UNROLL) * (1.0 / CH)
    scale = lax.rsqrt(spread + 1e-05)

    @pl.loop(0, 8, unroll=UNROLL)
    def _(g):
        rows = pl.ds(pl.multiple_of(g * 256, 256), 256)
        wide[rows, :] = ((recv[pl.ds(g * 16, 16)].astype(F32) - mean[None]) * scale[None]).reshape(256, L)


def finish(q, wide, weights, gate, base):
    shaped = jnp.concatenate(
        [wide[pl.ds(2 * q + e, CH, stride=S), :] for e in range(2)], axis=1
    ).astype(BF)
    branch = jnp.dot(weights[...], shaped, preferred_element_type=F32)
    return (base[q].astype(F32) + gate[q] * branch).astype(BF)


def kernel(
    pair_hbm, mask_hbm, in1_hbm, gate1_hbm, final1_hbm, in2_hbm, gate2_hbm, final2_hbm, out,
    pair, mask, in1, gate1, final1, in2, gate2, final2, copy_sems,
    base, normed, gate, wide, wide2, wt, ft, keep,
    send_l1, recv_l1, send_r1, recv_r1, send_t1, recv_t1, send_l2, recv_l2, send_r2, recv_r2, send_t2, recv_t2,
    lmat, rmat, turned, send_sems, recv_sems,
):
    torus = Torus()
    row, col = lax.axis_index("row"), lax.axis_index("col")
    sems = [(send_sems.at[k], recv_sems.at[k]) for k in range(6)]
    copies = [
        pltpu.make_async_copy(src, dst, copy_sems.at[k])
        for k, (src, dst) in enumerate(
            ((pair_hbm, pair), (mask_hbm, mask), (in1_hbm, in1), (gate1_hbm, gate1), (final1_hbm, final1),
             (in2_hbm, in2), (gate2_hbm, gate2), (final2_hbm, final2))
        )
    ]
    for copy in copies:
        copy.start()

    barrier = pltpu.get_barrier_semaphore()

    @pl.loop(1, DEVS)
    def _(t):
        pl.semaphore_signal(
            barrier, inc=1, device_id=lax.rem(torus.me + t, DEVS), device_id_type=LOGICAL
        )

    for copy in copies:
        copy.wait()

    for k, (a, b, c) in enumerate(((in1, gate1, final1), (in2, gate2, final2))):
        wt[k, 0 : 4 * CH] = a[...].astype(F32).T.astype(BF)
        wt[k, 4 * CH : 5 * CH] = b[...].astype(F32).T.astype(BF)
        ft[k] = c[...].astype(F32).T.astype(BF)

    held = mask[...].astype(F32)
    spot = lax.broadcasted_iota(jnp.int32, (S, 512), 1)
    line = lax.broadcasted_iota(jnp.int32, (S, 512), 0)
    first = jnp.sum(jnp.where(spot == row * 32 + line, held, 0.0), axis=1, keepdims=True)
    second = jnp.sum(jnp.where(spot == row * 32 + 16 + line, held, 0.0), axis=1, keepdims=True)
    spot = lax.broadcasted_iota(jnp.int32, (L, 512), 1)
    line = lax.broadcasted_iota(jnp.int32, (L, 512), 0)
    across = jnp.sum(
        jnp.where(spot == col * 64 + lax.rem(line, 64), held, 0.0), axis=1, keepdims=True
    )
    across = jnp.broadcast_to(across, (L, L)).T[0:S]
    lane = lax.broadcasted_iota(jnp.int32, (S, L), 1)
    keep[...] = jnp.where(lane < 64, first, second) * across

    @pl.loop(0, S // 2, unroll=UNROLL)
    def _(q):
        values = jnp.concatenate(
            [pair[2 * q], pair[S + 2 * q], pair[2 * q + 1], pair[S + 2 * q + 1]], axis=0
        )
        values = values.astype(F32).T
        base[q] = values.astype(BF)
        normed[q] = norm0(values).astype(BF)

    edge(1, wt.at[0], normed, keep, wide, send_r1)
    pl.semaphore_wait(barrier, DEVS - 1)
    exchange(torus, send_r1, recv_r1, sems[1])
    edge(0, wt.at[0], normed, keep, wide, send_l1)
    exchange(torus, send_l1, recv_l1, sems[0])
    gates(wt.at[0], normed, gate)
    wait_all(recv_r1, sems[1][1])
    gather(recv_r1, rmat, turned)
    wait_all(recv_l1, sems[0][1])
    gather(recv_l1, lmat, None)
    multiply(torus, lmat, turned, send_t1, recv_t1, sems[2])
    wait_all(recv_t1, sems[2][1])
    shape(recv_t1, wide)

    @pl.loop(0, S // 2, unroll=UNROLL)
    def _(q):
        middle = finish(q, wide, ft.at[0], gate, base)
        base[q] = middle
        normed[q] = norm0(middle.astype(F32)).astype(BF)

    edge(0, wt.at[1], normed, keep, wide2, send_l2)
    exchange(torus, send_l2, recv_l2, sems[3])
    edge(1, wt.at[1], normed, keep, wide, send_r2)
    exchange(torus, send_r2, recv_r2, sems[4])
    gates(wt.at[1], normed, gate)
    wait_all(recv_l2, sems[3][1])
    gather(recv_l2, lmat, turned)
    wait_all(recv_r2, sems[4][1])
    gather(recv_r2, rmat, None)
    multiply(torus, turned, rmat, send_t2, recv_t2, sems[5])
    wait_all(recv_t2, sems[5][1])
    shape(recv_t2, wide)

    @pl.loop(0, S // 2, unroll=UNROLL)
    def _(q):
        done = finish(q, wide, ft.at[1], gate, base).astype(F32).T.astype(BF)
        out[2 * q] = done[0:64]
        out[S + 2 * q] = done[64:128]
        out[2 * q + 1] = done[128:192]
        out[S + 2 * q + 1] = done[192:256]

    for k, ref in enumerate((send_l1, send_r1, send_t1, send_l2, send_r2, send_t2)):
        wait_all(ref, sems[k][0])


def shards(*args):
    pair, mask, *weights = args
    operands = (pair, mask.reshape(1, 512), *weights)
    tiles = pltpu.VMEM((DEVS, S, L), BF)
    square = pltpu.VMEM((512, 512), BF)
    return pl.pallas_call(
        kernel,
        out_shape=jax.ShapeDtypeStruct(pair.shape, BF),
        in_specs=[pl.BlockSpec(memory_space=pltpu.HBM)] * 8,
        out_specs=pl.BlockSpec(memory_space=pltpu.VMEM),
        scratch_shapes=[
            *[pltpu.VMEM(v.shape, v.dtype) for v in operands],
            pltpu.SemaphoreType.DMA((8,)),
            pltpu.VMEM((S // 2, CH, 2 * L), BF),
            pltpu.VMEM((S // 2, CH, 2 * L), BF),
            pltpu.VMEM((S // 2, CH, 2 * L), F32),
            pltpu.VMEM((CH * S, L), F32),
            pltpu.VMEM((CH * S, L), F32),
            pltpu.VMEM((2, 5 * CH, CH), BF),
            pltpu.VMEM((2, CH, CH), BF),
            pltpu.VMEM((S, L), F32),
            *[tiles] * 12,
            square, square, square,
            pltpu.SemaphoreType.DMA((6,)),
            pltpu.SemaphoreType.DMA((6,)),
        ],
        compiler_params=pltpu.CompilerParams(
            collective_id=0, has_side_effects=True, vmem_limit_bytes=VMEM_BYTES
        ),
    )(*operands)


def solution(mesh):
    return jax.shard_map(
        shards,
        mesh=mesh,
        in_specs=(P("row", "col", None), P(), P(), P(), P(), P(), P(), P()),
        out_specs=P("row", "col", None),
        check_vma=False,
    )
```

time: 86.5 us -> 65.1 us (0.75)
  Pallas kernels: 78.6 us -> 63 us
  local copies, waits for them, and re-layouts: 7.35 us -> 1.87 us
    pallas_call x1, Pallas kernels: 78.6 us -> 63 us  [shards(): pl.pallas_call(kernel, out_shape=jax.ShapeDtypeStruct(pair.shape, BF), in...]
    unnamed x17 -> x1, local copies, waits for them, and re-layouts: 7.35 us -> 1.87 us
where the time goes in v2:
time: 65.1 us; the launch traced here: 64.9 us
  Pallas kernels  63 us (97%)
  local copies, waits for them, and re-layouts  1.87 us (3%)
    pallas_call x1, Pallas kernels, shards(): pl.pallas_call(kernel, out_shape=jax.ShapeDtypeStruct(pair.shape, BF), in...  63 us
    unnamed x1, local copies, waits for them, and re-layouts  1.87 us

profile of v2, /device:TPU:1, one launch (start us, length us, event | category | flops | bytes accessed | tf_op | source)
XLA Modules:
  0.0 64.9 jit_solution(3997989847804134510)
XLA Ops:
  0.0 63.0 %shard_map.82 = bf16[32,64,128]{2,1,0:T(8,128)(2,1)} custom-call(bf16[32,64,128]{2,1,0:T(8,128)(2,1)} %pair_hbm.1, s32[1,512]{1,0:T(1,128)} %bitcast.1, bf16[128,512]{1,0:T(8,128)(2,1)} %in1_hbm.1, bf16[128,128]{1,0:T(8,128)(2,1)} %gate1_hbm.1, bf16[128,128]{1,0:T(8,128)(2,1)} %final1_hbm.1, bf16[128,512]{1,0:T(8,128)(2,1)} %in2_hbm.1, ...), custom_call_target="tpu_custom_call" | custom-call | tf_op jit(solution)/shard_map/pallas_call | solution.py:284
  63.0 1.9 %copy.10 = bf16[32,64,128]{2,1,0:T(8,128)(2,1)} copy(bf16[32,64,128]{2,1,0:T(8,128)(2,1)} %shard_map.82) | data formatting | bytes 1048576

commit v3 on v2

--- a/solution.py
+++ b/solution.py
@@ -5,7 +5,7 @@
 from jax.experimental.pallas import tpu as pltpu
 from jax.sharding import PartitionSpec as P
 
-VMEM_BYTES = 63 * 2**20
+VMEM_BYTES = 32 * 2**20
 UNROLL = True
 LOGICAL = pl.DeviceIdType.LOGICAL
 CH = 128
@@ -16,14 +16,15 @@
 COLS = 8
 BF = jnp.bfloat16
 F32 = jnp.float32
-PLANE = sorted(
-    ((dx, dy, dc) for dx in range(4) for dy in range(4) for dc in range(2)),
-    key=lambda o: -min(o[0], 4 - o[0]) - min(o[1], 4 - o[1]),
-)
 ORDER = sorted(
     ((dx, dy, dz, dc) for dz in range(4) for dy in range(4) for dx in range(4) for dc in range(2)),
     key=lambda o: -sum(min(v, 4 - v) for v in o[:3]),
-)[:-2] + [(0, 0, 0, 1)]
+)
+ORDER.remove((0, 0, 0, 0))
+
+
+def half(axis, odd):
+    return [o for o in ORDER if o[axis] % 2 == odd]
 
 
 class Torus:
@@ -71,15 +72,14 @@
     ).start()
 
 
-def exchange(torus, send, recv, sems):
-    for offset in ORDER:
+def exchange(torus, offsets, send, recv, sems):
+    for offset in offsets:
         push(torus, torus.at(*offset), send, recv, sems)
-    recv[torus.me] = send[torus.me]
-
-
-def wait_all(ref, sem):
-    others = ref.at[pl.ds(0, DEVS - 1)]
-    pltpu.make_async_copy(others, others, sem).wait()
+
+
+def wait_for(ref, count, sem):
+    some = ref.at[pl.ds(0, count)]
+    pltpu.make_async_copy(some, some, sem).wait()
 
 
 def edge(side, weights, normed, keep, wide, send):
@@ -107,42 +107,62 @@
         )
 
 
-def gather(recv, mat, turned):
-    @pl.loop(0, ROWS, unroll=UNROLL)
-    def _(r):
-        at = pl.multiple_of(r * 2 * S, 2 * S)
+def gather(recv, mat):
+    for r in range(ROWS):
         for p in range(COLS // 2):
             low, high = swap_halves(recv[r * COLS + 2 * p], recv[r * COLS + 2 * p + 1])
-            mat[pl.ds(at, S), p * L : (p + 1) * L] = low
-            mat[pl.ds(at + S, S), p * L : (p + 1) * L] = high
-
-    if turned is not None:
-        for m in range(4):
-            for n in range(4):
-                turned[n * L : (n + 1) * L, m * L : (m + 1) * L] = mat[
-                    m * L : (m + 1) * L, n * L : (n + 1) * L
-                ].T
-
-
-def multiply(torus, lhs, rhs, send, recv, sems):
-    for dz in (2, 1, 3, 0):
-        plane = torus.planes[dz]
-        total = jnp.dot(
-            lhs[pl.ds(pl.multiple_of(plane * L, L), L), :], rhs[...], preferred_element_type=F32
-        ).astype(BF)
+            mat[r * 2 * S : r * 2 * S + S, p * L : (p + 1) * L] = low
+            mat[r * 2 * S + S : (r + 1) * 2 * S, p * L : (p + 1) * L] = high
+
+
+def turn(mat, turned):
+    for m in range(4):
+        for n in range(4):
+            turned[n * L : (n + 1) * L, m * L : (m + 1) * L] = mat[
+                m * L : (m + 1) * L, n * L : (n + 1) * L
+            ].T
+
+
+def outgoing(torus, odd, recv_l, lhs, rhs, send):
+    planes = [torus.planes[odd], torus.planes[odd + 2]]
+    for n, plane in enumerate(planes):
         for k in range(4):
             for p in range(COLS // 2):
+                at = plane * 32 + k * COLS + 2 * p
+                low, high = swap_halves(recv_l[at], recv_l[at + 1])
+                row = n * L + k * 2 * S
+                lhs[row : row + S, p * L : (p + 1) * L] = low
+                lhs[row + S : row + 2 * S, p * L : (p + 1) * L] = high
+    total = jnp.dot(lhs[...], rhs[...], preferred_element_type=F32).astype(BF)
+    for n, plane in enumerate(planes):
+        for k in range(4):
+            row = n * L + k * 2 * S
+            for p in range(COLS // 2):
                 cols = slice(p * L, (p + 1) * L)
+                low, high = swap_halves(total[row : row + S, cols], total[row + S : row + 2 * S, cols])
+                at = plane * 32 + k * COLS + 2 * p
+                send[at] = low
+                send[at + 1] = high
+
+
+def incoming(torus, odd, recv_r, lhs, rhs, send):
+    for r in range(ROWS):
+        for n in range(2):
+            at = r * COLS + torus.xs[odd + 2 * n]
+            low, high = swap_halves(recv_r[at], recv_r[at + 1])
+            rhs[r * 2 * S : r * 2 * S + S, n * L : (n + 1) * L] = low
+            rhs[r * 2 * S + S : (r + 1) * 2 * S, n * L : (n + 1) * L] = high
+    for m in range(2):
+        total = jnp.dot(lhs[m * 256 : (m + 1) * 256, :], rhs[...], preferred_element_type=F32).astype(BF)
+        for k in range(8):
+            for n in range(2):
+                cols = slice(n * L, (n + 1) * L)
                 low, high = swap_halves(
-                    total[k * 2 * S : k * 2 * S + S, cols],
-                    total[k * 2 * S + S : (k + 1) * 2 * S, cols],
+                    total[k * 2 * S : k * 2 * S + S, cols], total[k * 2 * S + S : (k + 1) * 2 * S, cols]
                 )
-                send[plane * 32 + k * COLS + 2 * p] = low
-                send[plane * 32 + k * COLS + 2 * p + 1] = high
-        for dx, dy, dc in PLANE:
-            if (dx, dy, dz, dc) != (0, 0, 0, 0):
-                push(torus, torus.at(dx, dy, dz, dc), send, recv, sems)
-    recv[torus.me] = send[torus.me]
+                at = (m * 8 + k) * COLS + torus.xs[odd + 2 * n]
+                send[at] = low
+                send[at + 1] = high
 
 
 def shape(recv, wide):
@@ -177,11 +197,10 @@
     pair, mask, in1, gate1, final1, in2, gate2, final2, copy_sems,
     base, normed, gate, wide, wide2, wt, ft, keep,
     send_l1, recv_l1, send_r1, recv_r1, send_t1, recv_t1, send_l2, recv_l2, send_r2, recv_r2, send_t2, recv_t2,
-    lmat, rmat, turned, send_sems, recv_sems,
+    mat, turned, part_a, part_b, send_sems, recv_sems,
 ):
     torus = Torus()
     row, col = lax.axis_index("row"), lax.axis_index("col")
-    sems = [(send_sems.at[k], recv_sems.at[k]) for k in range(6)]
     copies = [
         pltpu.make_async_copy(src, dst, copy_sems.at[k])
         for k, (src, dst) in enumerate(
@@ -203,10 +222,7 @@
     for copy in copies:
         copy.wait()
 
-    for k, (a, b, c) in enumerate(((in1, gate1, final1), (in2, gate2, final2))):
-        wt[k, 0 : 4 * CH] = a[...].astype(F32).T.astype(BF)
-        wt[k, 4 * CH : 5 * CH] = b[...].astype(F32).T.astype(BF)
-        ft[k] = c[...].astype(F32).T.astype(BF)
+    wt[0, 2 * CH : 4 * CH] = in1[:, 2 * CH : 4 * CH].T
 
     held = mask[...].astype(F32)
     spot = lax.broadcasted_iota(jnp.int32, (S, 512), 1)
@@ -233,16 +249,32 @@
 
     edge(1, wt.at[0], normed, keep, wide, send_r1)
     pl.semaphore_wait(barrier, DEVS - 1)
-    exchange(torus, send_r1, recv_r1, sems[1])
+    sems = [(send_sems.at[k], recv_sems.at[k]) for k in range(10)]
+    exchange(torus, ORDER, send_r1, recv_r1, sems[0])
+    wt[0, 0 : 2 * CH] = in1[:, 0 : 2 * CH].T
     edge(0, wt.at[0], normed, keep, wide, send_l1)
-    exchange(torus, send_l1, recv_l1, sems[0])
+    for odd in range(2):
+        exchange(torus, half(2, odd), send_l1, recv_l1, sems[1 + odd])
+    recv_r1[torus.me] = send_r1[torus.me]
+    recv_l1[torus.me] = send_l1[torus.me]
+
+    wt[0, 4 * CH : 5 * CH] = gate1[...].T
+    wt[1, 0 : 4 * CH] = in2[...].T
+    wt[1, 4 * CH : 5 * CH] = gate2[...].T
+    ft[0] = final1[...].T
+    ft[1] = final2[...].T
     gates(wt.at[0], normed, gate)
-    wait_all(recv_r1, sems[1][1])
-    gather(recv_r1, rmat, turned)
-    wait_all(recv_l1, sems[0][1])
-    gather(recv_l1, lmat, None)
-    multiply(torus, lmat, turned, send_t1, recv_t1, sems[2])
-    wait_all(recv_t1, sems[2][1])
+
+    wait_for(recv_r1, DEVS - 1, sems[0][1])
+    gather(recv_r1, mat)
+    turn(mat, turned)
+    for odd in range(2):
+        wait_for(recv_l1, len(half(2, odd)), sems[1 + odd][1])
+        outgoing(torus, odd, recv_l1, (part_a, part_b)[odd], turned, send_t1)
+        exchange(torus, half(2, odd), send_t1, recv_t1, sems[3 + odd])
+    recv_t1[torus.me] = send_t1[torus.me]
+    for odd in range(2):
+        wait_for(recv_t1, len(half(2, odd)), sems[3 + odd][1])
     shape(recv_t1, wide)
 
     @pl.loop(0, S // 2, unroll=UNROLL)
@@ -252,16 +284,25 @@
         normed[q] = norm0(middle.astype(F32)).astype(BF)
 
     edge(0, wt.at[1], normed, keep, wide2, send_l2)
-    exchange(torus, send_l2, recv_l2, sems[3])
+    exchange(torus, ORDER, send_l2, recv_l2, sems[5])
     edge(1, wt.at[1], normed, keep, wide, send_r2)
-    exchange(torus, send_r2, recv_r2, sems[4])
+    for odd in range(2):
+        exchange(torus, half(0, odd), send_r2, recv_r2, sems[6 + odd])
+    recv_l2[torus.me] = send_l2[torus.me]
+    recv_r2[torus.me] = send_r2[torus.me]
+
     gates(wt.at[1], normed, gate)
-    wait_all(recv_l2, sems[3][1])
-    gather(recv_l2, lmat, turned)
-    wait_all(recv_r2, sems[4][1])
-    gather(recv_r2, rmat, None)
-    multiply(torus, turned, rmat, send_t2, recv_t2, sems[5])
-    wait_all(recv_t2, sems[5][1])
+
+    wait_for(recv_l2, DEVS - 1, sems[5][1])
+    gather(recv_l2, mat)
+    turn(mat, turned)
+    for odd in range(2):
+        wait_for(recv_r2, len(half(0, odd)), sems[6 + odd][1])
+        incoming(torus, odd, recv_r2, turned, (mat.at[:, 0:256], mat.at[:, 256:512])[odd], send_t2)
+        exchange(torus, half(0, odd), send_t2, recv_t2, sems[8 + odd])
+    recv_t2[torus.me] = send_t2[torus.me]
+    for odd in range(2):
+        wait_for(recv_t2, len(half(0, odd)), sems[8 + odd][1])
     shape(recv_t2, wide)
 
     @pl.loop(0, S // 2, unroll=UNROLL)
@@ -272,18 +313,22 @@
         out[2 * q + 1] = done[128:192]
         out[S + 2 * q + 1] = done[192:256]
 
-    for k, ref in enumerate((send_l1, send_r1, send_t1, send_l2, send_r2, send_t2)):
-        wait_all(ref, sems[k][0])
+    for k, ref in ((0, send_r1), (5, send_l2)):
+        wait_for(ref, DEVS - 1, sems[k][0])
+    for k, ref in ((1, send_l1), (3, send_t1), (6, send_r2), (8, send_t2)):
+        for odd in range(2):
+            wait_for(ref, len(half(0, odd)), sems[k + odd][0])
 
 
 def shards(*args):
     pair, mask, *weights = args
     operands = (pair, mask.reshape(1, 512), *weights)
+    operands = [pltpu.with_memory_space_constraint(v, pltpu.HBM) for v in operands]
     tiles = pltpu.VMEM((DEVS, S, L), BF)
     square = pltpu.VMEM((512, 512), BF)
     return pl.pallas_call(
         kernel,
-        out_shape=jax.ShapeDtypeStruct(pair.shape, BF),
+        out_shape=pltpu.VMEM(pair.shape, BF),
         in_specs=[pl.BlockSpec(memory_space=pltpu.HBM)] * 8,
         out_specs=pl.BlockSpec(memory_space=pltpu.VMEM),
         scratch_shapes=[
@@ -298,9 +343,11 @@
             pltpu.VMEM((2, CH, CH), BF),
             pltpu.VMEM((S, L), F32),
             *[tiles] * 12,
-            square, square, square,
-            pltpu.SemaphoreType.DMA((6,)),
-            pltpu.SemaphoreType.DMA((6,)),
+            square, square,
+            pltpu.VMEM((256, 512), BF),
+            pltpu.VMEM((256, 512), BF),
+            pltpu.SemaphoreType.DMA((10,)),
+            pltpu.SemaphoreType.DMA((10,)),
         ],
         compiler_params=pltpu.CompilerParams(
             collective_id=0, has_side_effects=True, vmem_limit_bytes=VMEM_BYTES

time: 65.1 us -> 61.3 us (0.942)
  Pallas kernels: 63 us -> 60.4 us
  local copies, waits for them, and re-layouts: 1.87 us -> 0.8 us
    pallas_call x1, Pallas kernels: 63 us -> 60.4 us  [shards(): pl.pallas_call(kernel, out_shape=pltpu.VMEM(pair.shape, BF), in_specs=[pl...]
    unnamed x1, local copies, waits for them, and re-layouts: 1.87 us -> 0.8 us
where the time goes in v3:
time: 61.3 us; the launch traced here: 61.2 us
  Pallas kernels  60.4 us (99%)
  local copies, waits for them, and re-layouts  0.8 us (1%)
    pallas_call x1, Pallas kernels, shards(): pl.pallas_call(kernel, out_shape=pltpu.VMEM(pair.shape, BF), in_specs=[pl...  60.4 us

profile of v3, /device:TPU:1, one launch (start us, length us, event | category | flops | bytes accessed | tf_op | source)
XLA Modules:
  0.0 61.2 jit_solution(15981367715335401031)
XLA Ops:
  0.0 60.4 %shard_map.82 = bf16[32,64,128]{2,1,0:T(8,128)(2,1)S(1)} custom-call(bf16[32,64,128]{2,1,0:T(8,128)(2,1)} %pair_hbm.1, s32[1,512]{1,0:T(1,128)} %bitcast.1, bf16[128,512]{1,0:T(8,128)(2,1)} %in1_hbm.1, bf16[128,128]{1,0:T(8,128)(2,1)} %gate1_hbm.1, bf16[128,128]{1,0:T(8,128)(2,1)} %final1_hbm.1, bf16[128,512]{1,0:T(8,128)(2,1)} %in2_hbm.1, ...), custom_call_target="tpu_custom_call" | custom-call | tf_op jit(solution)/shard_map/pallas_call | solution.py:329
  60.4 0.8 %copy.10 = bf16[32,64,128]{2,1,0:T(8,128)(2,1)} copy(bf16[32,64,128]{2,1,0:T(8,128)(2,1)S(1)} %shard_map.82) | data formatting | bytes 1048576

commit v4 on v3

--- a/solution.py
+++ b/solution.py
@@ -43,8 +43,8 @@
         return self.planes[dz] * 32 + self.ys[dy] + self.xs[dx] + self.cs[dc]
 
 
-def sigmoid(v):
-    return 0.5 * jnp.tanh(0.5 * v) + 0.5
+def turn_half(weights):
+    return (weights.astype(F32) * 0.5).astype(BF).T
 
 
 def norm0(v):
@@ -89,7 +89,7 @@
             weights[side * 2 * CH : (side + 1) * 2 * CH, :], normed[q], preferred_element_type=F32
         )
         mask = jnp.concatenate([keep[pl.ds(2 * q, 1), :], keep[pl.ds(2 * q + 1, 1), :]], axis=1)
-        value = mask * sigmoid(proj[0:CH]) * proj[CH : 2 * CH]
+        value = mask * (jnp.tanh(proj[0:CH]) + 1.0) * proj[CH : 2 * CH]
         for e in range(2):
             wide[pl.ds(2 * q + e, CH, stride=S), :] = value[:, e * L : (e + 1) * L]
 
@@ -102,9 +102,8 @@
 def gates(weights, normed, gate):
     @pl.loop(0, S // 2, unroll=UNROLL)
     def _(q):
-        gate[q] = sigmoid(
-            jnp.dot(weights[4 * CH : 5 * CH, :], normed[q], preferred_element_type=F32)
-        )
+        proj = jnp.dot(weights[4 * CH : 5 * CH, :], normed[q], preferred_element_type=F32)
+        gate[q] = jnp.tanh(proj) + 1.0
 
 
 def gather(recv, mat):
@@ -165,29 +164,49 @@
                 send[at + 1] = high
 
 
-def shape(recv, wide):
-    total = lax.fori_loop(
-        0, 8, lambda g, a: a + jnp.sum(recv[pl.ds(g * 16, 16)].astype(F32), axis=0), jnp.zeros((S, L), F32), unroll=UNROLL
-    )
-    mean = total * (1.0 / CH)
-
-    def squares(g, a):
-        center = recv[pl.ds(g * 16, 16)].astype(F32) - mean[None]
-        return a + jnp.sum(center * center, axis=0)
-
-    spread = lax.fori_loop(0, 8, squares, jnp.zeros((S, L), F32), unroll=UNROLL) * (1.0 / CH)
-    scale = lax.rsqrt(spread + 1e-05)
-
-    @pl.loop(0, 8, unroll=UNROLL)
-    def _(g):
-        rows = pl.ds(pl.multiple_of(g * 256, 256), 256)
-        wide[rows, :] = ((recv[pl.ds(g * 16, 16)].astype(F32) - mean[None]) * scale[None]).reshape(256, L)
-
-
-def finish(q, wide, weights, gate, base):
-    shaped = jnp.concatenate(
-        [wide[pl.ds(2 * q + e, CH, stride=S), :] for e in range(2)], axis=1
-    ).astype(BF)
+def spread(recv, starts, count, wide, shift):
+    total = jnp.zeros((S, L), F32)
+    square = jnp.zeros((S, L), F32)
+    for at in starts:
+        tiles = recv[pl.ds(at, count)].astype(F32)
+        wide[pl.ds(pl.multiple_of(at * S, count * S), count * S), :] = tiles.reshape(count * S, L)
+        if shift is not None:
+            tiles = tiles - shift[None]
+            square = square + jnp.sum(tiles * tiles, axis=0)
+        total = total + jnp.sum(tiles, axis=0)
+    mean = total * (2.0 / CH)
+    if shift is None:
+        for at in starts:
+            tiles = recv[pl.ds(at, count)].astype(F32) - mean[None]
+            square = square + jnp.sum(tiles * tiles, axis=0)
+    return mean, square
+
+
+def z_starts(torus, odd):
+    return [torus.planes[odd + 2 * n] * 32 + k * 16 for n in range(2) for k in range(2)]
+
+
+def x_starts(torus, odd):
+    return [r * COLS + torus.xs[odd + 2 * n] for r in range(ROWS) for n in range(2)]
+
+
+def statistics(torus, axis, recv, sems, wide, stats):
+    starts, count = (z_starts, 16) if axis == 2 else (x_starts, 2)
+    wait_for(recv, len(half(axis, 0)), sems[0][1])
+    mean, square = spread(recv, starts(torus, 0), count, wide, None)
+    wait_for(recv, len(half(axis, 1)), sems[1][1])
+    apart, more = spread(recv, starts(torus, 1), count, wide, mean)
+    spread_all = (square + more - (CH / 4.0) * apart * apart) * (1.0 / CH)
+    stats[0] = mean + 0.5 * apart
+    stats[1] = lax.rsqrt(spread_all + 1e-05)
+
+
+def finish(q, wide, stats, weights, gate, base):
+    shaped = []
+    for s in (2 * q, 2 * q + 1):
+        row = pl.ds(s, 1)
+        shaped.append((wide[pl.ds(s, CH, stride=S), :] - stats[0, row, :]) * stats[1, row, :])
+    shaped = jnp.concatenate(shaped, axis=1).astype(BF)
     branch = jnp.dot(weights[...], shaped, preferred_element_type=F32)
     return (base[q].astype(F32) + gate[q] * branch).astype(BF)
 
@@ -195,7 +214,7 @@
 def kernel(
     pair_hbm, mask_hbm, in1_hbm, gate1_hbm, final1_hbm, in2_hbm, gate2_hbm, final2_hbm, out,
     pair, mask, in1, gate1, final1, in2, gate2, final2, copy_sems,
-    base, normed, gate, wide, wide2, wt, ft, keep,
+    base, normed, gate, wide, wide2, wt, ft, keep, stats,
     send_l1, recv_l1, send_r1, recv_r1, send_t1, recv_t1, send_l2, recv_l2, send_r2, recv_r2, send_t2, recv_t2,
     mat, turned, part_a, part_b, send_sems, recv_sems,
 ):
@@ -222,7 +241,7 @@
     for copy in copies:
         copy.wait()
 
-    wt[0, 2 * CH : 4 * CH] = in1[:, 2 * CH : 4 * CH].T
+    wt[0, 2 * CH : 4 * CH] = turn_half(in1[:, 2 * CH : 4 * CH])
 
     held = mask[...].astype(F32)
     spot = lax.broadcasted_iota(jnp.int32, (S, 512), 1)
@@ -243,26 +262,26 @@
         values = jnp.concatenate(
             [pair[2 * q], pair[S + 2 * q], pair[2 * q + 1], pair[S + 2 * q + 1]], axis=0
         )
-        values = values.astype(F32).T
-        base[q] = values.astype(BF)
-        normed[q] = norm0(values).astype(BF)
+        values = values.T
+        base[q] = values
+        normed[q] = norm0(values.astype(F32)).astype(BF)
 
     edge(1, wt.at[0], normed, keep, wide, send_r1)
     pl.semaphore_wait(barrier, DEVS - 1)
     sems = [(send_sems.at[k], recv_sems.at[k]) for k in range(10)]
     exchange(torus, ORDER, send_r1, recv_r1, sems[0])
-    wt[0, 0 : 2 * CH] = in1[:, 0 : 2 * CH].T
+    wt[0, 0 : 2 * CH] = turn_half(in1[:, 0 : 2 * CH])
     edge(0, wt.at[0], normed, keep, wide, send_l1)
     for odd in range(2):
         exchange(torus, half(2, odd), send_l1, recv_l1, sems[1 + odd])
     recv_r1[torus.me] = send_r1[torus.me]
     recv_l1[torus.me] = send_l1[torus.me]
 
-    wt[0, 4 * CH : 5 * CH] = gate1[...].T
-    wt[1, 0 : 4 * CH] = in2[...].T
-    wt[1, 4 * CH : 5 * CH] = gate2[...].T
-    ft[0] = final1[...].T
-    ft[1] = final2[...].T
+    wt[0, 4 * CH : 5 * CH] = turn_half(gate1[...])
+    wt[1, 0 : 4 * CH] = turn_half(in2[...])
+    wt[1, 4 * CH : 5 * CH] = turn_half(gate2[...])
+    ft[0] = turn_half(final1[...])
+    ft[1] = turn_half(final2[...])
     gates(wt.at[0], normed, gate)
 
     wait_for(recv_r1, DEVS - 1, sems[0][1])
@@ -273,13 +292,11 @@
         outgoing(torus, odd, recv_l1, (part_a, part_b)[odd], turned, send_t1)
         exchange(torus, half(2, odd), send_t1, recv_t1, sems[3 + odd])
     recv_t1[torus.me] = send_t1[torus.me]
-    for odd in range(2):
-        wait_for(recv_t1, len(half(2, odd)), sems[3 + odd][1])
-    shape(recv_t1, wide)
-
-    @pl.loop(0, S // 2, unroll=UNROLL)
-    def _(q):
-        middle = finish(q, wide, ft.at[0], gate, base)
+    statistics(torus, 2, recv_t1, sems[3:5], wide, stats)
+
+    @pl.loop(0, S // 2, unroll=UNROLL)
+    def _(q):
+        middle = finish(q, wide, stats, ft.at[0], gate, base)
         base[q] = middle
         normed[q] = norm0(middle.astype(F32)).astype(BF)
 
@@ -301,13 +318,11 @@
         incoming(torus, odd, recv_r2, turned, (mat.at[:, 0:256], mat.at[:, 256:512])[odd], send_t2)
         exchange(torus, half(0, odd), send_t2, recv_t2, sems[8 + odd])
     recv_t2[torus.me] = send_t2[torus.me]
-    for odd in range(2):
-        wait_for(recv_t2, len(half(0, odd)), sems[8 + odd][1])
-    shape(recv_t2, wide)
-
-    @pl.loop(0, S // 2, unroll=UNROLL)
-    def _(q):
-        done = finish(q, wide, ft.at[1], gate, base).astype(F32).T.astype(BF)
+    statistics(torus, 0, recv_t2, sems[8:10], wide, stats)
+
+    @pl.loop(0, S // 2, unroll=UNROLL)
+    def _(q):
+        done = finish(q, wide, stats, ft.at[1], gate, base).T
         out[2 * q] = done[0:64]
         out[S + 2 * q] = done[64:128]
         out[2 * q + 1] = done[128:192]
@@ -342,6 +357,7 @@
             pltpu.VMEM((2, 5 * CH, CH), BF),
             pltpu.VMEM((2, CH, CH), BF),
             pltpu.VMEM((S, L), F32),
+            pltpu.VMEM((2, S, L), F32),
             *[tiles] * 12,
             square, square,
             pltpu.VMEM((256, 512), BF),

time: 61.3 us -> 60.9 us (level)
  no operation moved by 1% of the time
where the time goes in v4:
time: 60.9 us; the launch traced here: 60.8 us
  Pallas kernels  60 us (99%)
  local copies, waits for them, and re-layouts  0.8 us (1%)
    pallas_call x1, Pallas kernels, shards(): pl.pallas_call(kernel, out_shape=pltpu.VMEM(pair.shape, BF), in_specs=[pl...  60 us

profile of v4, /device:TPU:1, one launch (start us, length us, event | category | flops | bytes accessed | tf_op | source)
XLA Modules:
  0.0 60.8 jit_solution(15233789573814615776)
XLA Ops:
  0.0 60.0 %shard_map.82 = bf16[32,64,128]{2,1,0:T(8,128)(2,1)S(1)} custom-call(bf16[32,64,128]{2,1,0:T(8,128)(2,1)} %pair_hbm.1, s32[1,512]{1,0:T(1,128)} %bitcast.1, bf16[128,512]{1,0:T(8,128)(2,1)} %in1_hbm.1, bf16[128,128]{1,0:T(8,128)(2,1)} %gate1_hbm.1, bf16[128,128]{1,0:T(8,128)(2,1)} %final1_hbm.1, bf16[128,512]{1,0:T(8,128)(2,1)} %in2_hbm.1, ...), custom_call_target="tpu_custom_call" | custom-call | tf_op jit(solution)/shard_map/pallas_call | solution.py:344
  60.0 0.8 %copy.10 = bf16[32,64,128]{2,1,0:T(8,128)(2,1)} copy(bf16[32,64,128]{2,1,0:T(8,128)(2,1)S(1)} %shard_map.82) | data formatting | bytes 1048576

commit v5 on v4

--- a/solution.py
+++ b/solution.py
@@ -34,10 +34,13 @@
         self.z = row // 4
         y = lax.rem(col, 2) * 2 + lax.rem(row // 2, 2)
         self.planes = [lax.rem(self.z + d, 4) for d in range(4)]
+        columns = [lax.rem(col // 2 + d, 4) for d in range(4)]
         ys = [lax.rem(y + d, 4) for d in range(4)]
         self.ys = [lax.rem(v, 2) * 16 + v // 2 for v in ys]
-        self.xs = [lax.rem(col // 2 + d, 4) * 2 for d in range(4)]
+        self.xs = [v * 2 for v in columns]
         self.cs = [lax.rem(lax.rem(row, 2) + d, 2) * 8 for d in range(2)]
+
+        self.late = ([jnp.minimum(v, 2) for v in columns], [jnp.minimum(v, 2) for v in ys], self.planes)
 
     def at(self, dx, dy, dz, dc):
         return self.planes[dz] * 32 + self.ys[dy] + self.xs[dx] + self.cs[dc]
@@ -75,6 +78,15 @@
 def exchange(torus, offsets, send, recv, sems):
     for offset in offsets:
         push(torus, torus.at(*offset), send, recv, sems)
+
+
+def exchange_some(torus, offsets, send, recv, sems, early):
+    for dx, dy, dz, dc in offsets:
+        late = torus.late[0][dx] + torus.late[1][dy] + torus.late[2][dz]
+
+        @pl.when(late <= 3 if early else late > 3)
+        def _(to=torus.at(dx, dy, dz, dc)):
+            push(torus, to, send, recv, sems)
 
 
 def wait_for(ref, count, sem):
@@ -316,7 +328,9 @@
     for odd in range(2):
         wait_for(recv_r2, len(half(0, odd)), sems[6 + odd][1])
         incoming(torus, odd, recv_r2, turned, (mat.at[:, 0:256], mat.at[:, 256:512])[odd], send_t2)
-        exchange(torus, half(0, odd), send_t2, recv_t2, sems[8 + odd])
+        exchange_some(torus, half(0, odd), send_t2, recv_t2, sems[8 + odd], True)
+    for odd in range(2):
+        exchange_some(torus, half(0, odd), send_t2, recv_t2, sems[8 + odd], False)
     recv_t2[torus.me] = send_t2[torus.me]
     statistics(torus, 0, recv_t2, sems[8:10], wide, stats)
 

time: 60.9 us -> 60.3 us (level)
    pallas_call x1, Pallas kernels: 60 us -> 59.4 us  [shards(): pl.pallas_call(kernel, out_shape=pltpu.VMEM(pair.shape, BF), in_specs=[pl...]
where the time goes in v5:
time: 60.3 us; the launch traced here: 60.2 us
  Pallas kernels  59.4 us (99%)
  local copies, waits for them, and re-layouts  0.8 us (1%)
    pallas_call x1, Pallas kernels, shards(): pl.pallas_call(kernel, out_shape=pltpu.VMEM(pair.shape, BF), in_specs=[pl...  59.4 us

profile of v5, /device:TPU:1, one launch (start us, length us, event | category | flops | bytes accessed | tf_op | source)
XLA Modules:
  0.0 60.2 jit_solution(7579393461595214406)
XLA Ops:
  0.0 59.4 %shard_map.82 = bf16[32,64,128]{2,1,0:T(8,128)(2,1)S(1)} custom-call(bf16[32,64,128]{2,1,0:T(8,128)(2,1)} %pair_hbm.1, s32[1,512]{1,0:T(1,128)} %bitcast.1, bf16[128,512]{1,0:T(8,128)(2,1)} %in1_hbm.1, bf16[128,128]{1,0:T(8,128)(2,1)} %gate1_hbm.1, bf16[128,128]{1,0:T(8,128)(2,1)} %final1_hbm.1, bf16[128,512]{1,0:T(8,128)(2,1)} %in2_hbm.1, ...), custom_call_target="tpu_custom_call" | custom-call | tf_op jit(solution)/shard_map/pallas_call | solution.py:358
  59.4 0.8 %copy.10 = bf16[32,64,128]{2,1,0:T(8,128)(2,1)} copy(bf16[32,64,128]{2,1,0:T(8,128)(2,1)S(1)} %shard_map.82) | data formatting | bytes 1048576

commit v6 on v5

--- a/solution.py
+++ b/solution.py
@@ -244,11 +244,8 @@
 
     barrier = pltpu.get_barrier_semaphore()
 
-    @pl.loop(1, DEVS)
-    def _(t):
-        pl.semaphore_signal(
-            barrier, inc=1, device_id=lax.rem(torus.me + t, DEVS), device_id_type=LOGICAL
-        )
+    for offset in ORDER:
+        pl.semaphore_signal(barrier, inc=1, device_id=torus.at(*offset), device_id_type=LOGICAL)
 
     for copy in copies:
         copy.wait()

time: 60.3 us -> 60.3 us (level)
  no operation moved by 1% of the time
where the time goes in v6:
time: 60.3 us; the launch traced here: 60.2 us
  Pallas kernels  59.4 us (99%)
  local copies, waits for them, and re-layouts  0.8 us (1%)
    pallas_call x1, Pallas kernels, shards(): pl.pallas_call(kernel, out_shape=pltpu.VMEM(pair.shape, BF), in_specs=[pl...  59.4 us

profile of v6, /device:TPU:1, one launch (start us, length us, event | category | flops | bytes accessed | tf_op | source)
XLA Modules:
  0.0 60.2 jit_solution(9057187390975953967)
XLA Ops:
  0.0 59.4 %shard_map.82 = bf16[32,64,128]{2,1,0:T(8,128)(2,1)S(1)} custom-call(bf16[32,64,128]{2,1,0:T(8,128)(2,1)} %pair_hbm.1, s32[1,512]{1,0:T(1,128)} %bitcast.1, bf16[128,512]{1,0:T(8,128)(2,1)} %in1_hbm.1, bf16[128,128]{1,0:T(8,128)(2,1)} %gate1_hbm.1, bf16[128,128]{1,0:T(8,128)(2,1)} %final1_hbm.1, bf16[128,512]{1,0:T(8,128)(2,1)} %in2_hbm.1, ...), custom_call_target="tpu_custom_call" | custom-call | tf_op jit(solution)/shard_map/pallas_call | solution.py:355
  59.4 0.8 %copy.10 = bf16[32,64,128]{2,1,0:T(8,128)(2,1)} copy(bf16[32,64,128]{2,1,0:T(8,128)(2,1)S(1)} %shard_map.82) | data formatting | bytes 1048576
